TPU v7x, 1024 devices: a whole 8x8x8 slice. The times are simulated.
1024 devices in a mesh: row: 8 (over x), col: 16 (over z, core), layer: 8 (over y).
Axes of the slice: x: 8, y: 8, z: 8, core: 2. Of those that a mesh axis runs over, the one named last changes fastest.
Arguments:
- three_centre: bfloat16 [2048, 48, 2048], P('layer', 'row', 'col'), may hold values from -6 to 6
- occ_density: bfloat16 [2048, 2048], P('col', ('row', 'layer')), may hold values from -1 to 1, as said below
- virt_density: bfloat16 [2048, 2048], P('layer', ('row', 'col')), may hold values from -1 to 1, as said below
- pair_mask: int32 [16, 16], replicated, may hold values 0 or 1
- occ_mask: int32 [16, 16], replicated, may hold values from 0 to 1, as said below
- virt_mask: int32 [16, 16], replicated, may hold values from 0 to 1, as said below
- block_sizes: int32 [16], replicated, may hold values from 64 to 128
Outputs:
- transformed: bfloat16 [2048, 48, 2048], P('layer', 'row', 'col')
Inputs may be any that keep to these rules, and one draw needn't show every extreme that they name: `occ_density`: symmetric. `virt_density`: symmetric. `occ_mask`: symmetric, ones on the diagonal. `virt_mask`: symmetric, ones on the diagonal.
All inputs are finite; a program needn't handle non-finite values.
Results may differ from a plain program's by a relative error of at most 0.0049.
Values may be sent and summed in bfloat16 or wider, within the bound.
A program may use at most 32 MiB of HBM per device.

v0:
```python
import jax
import jax.numpy as jnp
from jax import lax
from jax.sharding import PartitionSpec as P

BLOCK = 128


def spread(offset, number, block_sizes):
    positions = offset + jnp.arange(number, dtype=jnp.int32)
    owners = (
        positions[:, None] // BLOCK == jnp.arange(block_sizes.shape[0], dtype=jnp.int32)[None, :]
    )
    rows_hot = owners.astype(jnp.float32)
    length = jnp.sum(rows_hot * block_sizes.astype(jnp.float32)[None, :], axis=1)
    living = ((positions % BLOCK).astype(jnp.float32) < length).astype(jnp.float32)
    return (rows_hot, living)


def keep_table(mask_table, rows_hot, cols_hot):
    table_float = mask_table.astype(jnp.float32)
    inner = jnp.dot(rows_hot, table_float, precision=lax.Precision.HIGHEST)
    return jnp.dot(inner, cols_hot.T, precision=lax.Precision.HIGHEST)


def masked_density(density_shard, mask_table, block_sizes, row_offset, col_offset):
    rows_hot, rows_living = spread(row_offset, density_shard.shape[0], block_sizes)
    cols_hot, cols_living = spread(col_offset, density_shard.shape[1], block_sizes)
    keep_mask = (
        keep_table(mask_table, rows_hot, cols_hot) * rows_living[:, None] * cols_living[None, :]
    )
    return (density_shard.astype(jnp.float32) * keep_mask).astype(jnp.bfloat16)


def on_device(three_centre, occ_density, virt_density, pair_mask, occ_mask, virt_mask, block_sizes):
    mu_count, aux_count, nu_count = three_centre.shape
    mu_offset = lax.axis_index("layer") * mu_count
    nu_offset = lax.axis_index("col") * nu_count
    occ_shard = masked_density(
        occ_density,
        occ_mask,
        block_sizes,
        lax.axis_index("col") * occ_density.shape[0],
        lax.axis_index(("row", "layer")) * occ_density.shape[1],
    )
    occ_rows = lax.all_gather(occ_shard, ("row", "layer"), axis=1, tiled=True)
    virt_shard = masked_density(
        virt_density,
        virt_mask,
        block_sizes,
        lax.axis_index("layer") * virt_density.shape[0],
        lax.axis_index(("row", "col")) * virt_density.shape[1],
    )
    virt_rows = lax.all_gather(virt_shard, ("row", "col"), axis=1, tiled=True)
    mu_hot, mu_living = spread(mu_offset, mu_count, block_sizes)
    nu_hot, nu_living = spread(nu_offset, nu_count, block_sizes)
    pair_keep = keep_table(pair_mask, mu_hot, nu_hot) > 0.5
    pair_data = jnp.where(pair_keep[:, None, :], three_centre, jnp.zeros((), jnp.bfloat16))
    occ_half = jnp.einsum(
        "mpn,kn->mpk",
        lax.all_gather(pair_data, "col", axis=2, tiled=True),
        occ_rows,
        preferred_element_type=jnp.float32,
    ).astype(jnp.bfloat16)
    summed = jnp.einsum(
        "am,mpk->apk",
        virt_rows,
        lax.all_gather(occ_half, "layer", axis=0, tiled=True),
        preferred_element_type=jnp.float32,
    )
    return summed.astype(jnp.bfloat16)


def solution(mesh):
    placed = (
        P("layer", "row", "col"),
        P("col", ("row", "layer")),
        P("layer", ("row", "col")),
        P(),
        P(),
        P(),
        P(),
    )
    return jax.shard_map(
        on_device, mesh=mesh, in_specs=placed, out_specs=P("layer", "row", "col"), check_vma=False
    )
```

profile of v0, /device:TPU:1, one launch (start us, length us, event | category | flops | bytes accessed | tf_op | source)
XLA Modules:
  0.0 232.6 jit_solution(12692178575400505893)
XLA Ops:
  6.5 0.0 all-gather.6.cloned.1.call-start
  6.6 1.0 fusion.8
  7.6 0.2 convolution_compare_fusion
  7.8 1.8 broadcast_select_fusion
  9.5 0.0 all-gather.6.cloned.1.call-update
  9.6 0.0 all-gather.4.cloned.1.call-start
  9.6 0.7 convert_element_type.98
  10.3 0.2 select_reduce_fusion.3
  10.5 0.1 select_reduce_fusion
  10.6 1.0 fusion.9
  11.6 1.5 fusion.4
  13.1 0.0 all-gather.4.cloned.1.call-update
  13.1 0.0 all-gather.8.cloned.1.call-start
  13.2 0.1 select_reduce_fusion.2
  13.3 0.1 select_reduce_fusion.1
  13.4 1.0 fusion.10
  14.4 0.9 fusion.5
  15.3 41.8 %all_gather.14 = bf16[128,2048]{0,1:T(8,128)(2,1)S(1)} all-gather(bf16[128,32]{0,1:T(8,128)(2,1)S(1)} %fusion.5), channel_id=1, replica_groups=mesh['row'=8,'col'=16,'layer'=8] {'row','layer'}, dimensions={1}, use_global_device_ids=true | all-gather | bytes 532480 | tf_op jit(solution)/shard_map/all_gather | solution.py:46
  57.1 30.1 %all-gather.6.cloned.1.call-done = bf16[256,6,2048]{2,0,1:T(8,128)(2,1)} async-done(((bf16[256,6,128]{2,0,1:T(8,128)(2,1)}), bf16[256,6,2048]{2,0,1:T(8,128)(2,1)}) %all-gather.6.cloned.1.call-update) | async-done | bytes 6291472 | tf_op jit(solution)/shard_map/all_gather | solution.py:61
  87.2 5.3 %convolution_convert_fusion.1 = bf16[256,6,128]{2,0,1:T(8,128)(2,1)} fusion(bf16[256,6,2048]{2,0,1:T(8,128)(2,1)} %all-gather.6.cloned.1.call-done, bf16[128,2048]{0,1:T(8,128)(2,1)S(1)} %all_gather.14), kind=kOutput, calls=%fused_computation.1 | convolution fusion | flops 805502976 | bytes 7208960 | tf_op jit(solution)/shard_map/mpn,kn->mpk/dot_general | solution.py:59
  92.5 0.0 all-gather.8.cloned.1.call-update
  92.5 81.9 %all-gather.4.cloned.1.call-done = bf16[256,2048]{0,1:T(8,128)(2,1)} async-done(((bf16[256,16]{0,1:T(8,128)(2,1)}), bf16[256,2048]{0,1:T(8,128)(2,1)}) %all-gather.4.cloned.1.call-update) | async-done | bytes 1048592 | tf_op jit(solution)/shard_map/all_gather | solution.py:54
  174.4 47.6 %all-gather.8.cloned.1.call-done = bf16[2048,6,128]{2,0,1:T(8,128)(2,1)} async-done(((bf16[256,6,128]{2,0,1:T(8,128)(2,1)}), bf16[2048,6,128]{2,0,1:T(8,128)(2,1)}) %all-gather.8.cloned.1.call-update) | async-done | bytes 3145744 | tf_op jit(solution)/shard_map/all_gather | solution.py:68
  222.1 4.0 %convolution_convert_fusion = bf16[256,6,128]{2,0,1:T(8,128)(2,1)} fusion(bf16[2048,6,128]{2,0,1:T(8,128)(2,1)} %all-gather.8.cloned.1.call-done, bf16[256,2048]{0,1:T(8,128)(2,1)} %all-gather.4.cloned.1.call-done), kind=kOutput, calls=%fused_computation | convolution fusion | flops 805502976 | bytes 4587520 | tf_op jit(solution)/shard_map/am,mpk->apk/dot_general | solution.py:65
  (8 shorter events, 0.1 us)
Async XLA Ops:
  6.5 80.6 %all-gather.6.cloned.1.call-start = ((), (), s32[]{:S(2)}) async-start(), calls=%async_computation.1 | async-start | bytes 6684672 | tf_op jit(solution)/shard_map/all_gather | solution.py:61
  9.6 164.9 %all-gather.4.cloned.1.call-start = ((), (), s32[]{:S(2)}) async-start(), calls=%async_computation | async-start | bytes 1056768 | tf_op jit(solution)/shard_map/all_gather | solution.py:54
  13.1 208.9 %all-gather.8.cloned.1.call-start = ((), (), s32[]{:S(2)}) async-start(), calls=%async_computation.2 | async-start | bytes 3538944 | tf_op jit(solution)/shard_map/all_gather | solution.py:68
Sparse Core Ops, SparseCore 0:
  10.0 77.1 all-gather.5
  91.4 83.0 all-gather.3
  177.1 44.9 all-gather.7
where the time goes:
time: 233 us
  waiting for transfers between devices  160 us (69%)
  blocking collectives  41.8 us (18%)
  matrix products  14.9 us (6%)
  between operations  13.2 us (6%)
  other arithmetic  2.97 us (1%)
    all_gather x1, waiting for transfers between devices, on_device(): virt_rows = lax.all_gather(virt_shard, ('row', 'col'), axis=1, tiled=True)  81.9 us
    all_gather x1, waiting for transfers between devices, on_device(): lax.all_gather(occ_half, 'layer', axis=0, tiled=True)  47.6 us
    all_gather x1, blocking collectives, on_device(): occ_rows = lax.all_gather(occ_shard, ('row', 'layer'), axis=1, tiled=True)  41.8 us
    all_gather x1, waiting for transfers between devices, on_device(): lax.all_gather(pair_data, 'col', axis=2, tiled=True)  30.1 us
    dot_general x1, matrix products, on_device(): jnp.einsum('mpn,kn->mpk', lax.all_gather(pair_data, 'col', axis=2, tiled=...  5.33 us
  transfers between devices with their start and end apart: 3, of which 3 were waited for; matrix products, arithmetic and copies ran while one was open for 5% of the time, Pallas kernels for 0%

commit v1 on v0

v1 whole, which is shorter than its diff:
```python
import jax
import jax.numpy as jnp
from jax import lax
from jax.experimental import pallas as pl
from jax.experimental.pallas import tpu as pltpu
from jax.sharding import PartitionSpec as P

MESH = pl.DeviceIdType.MESH
BLOCK = 128
N = 8
RELATIVE = (0, -1, 1, -2, 2, -3, 3, 4)
PLACE = {0: 0, -1: 1, 1: 2, -2: 3, 2: 4, -3: 5, 3: 6, 4: 7, -4: 7}
STAGES = (((0, 1),), ((1, 2),), ((2, 3), (2, 4)))
EDGES = tuple(edge for stage in STAGES for edge in stage)


def kernel(
    x_hbm, occ_hbm, virt_hbm, pair_mask, occ_mask, virt_mask, sizes,
    out_hbm,
    x_raw, occ_raw, virt_raw, xa, xb, ha, gb, og, vs, vg, outs,
    load_sem, store_sem, first_send, first_recv, dens_send, dens_recv,
    ring_send, ring_recv, sib_send, sib_recv, vsib_send, vsib_recv,
):
    x, col, y = lax.axis_index("row"), lax.axis_index("col"), lax.axis_index("layer")
    z, core = col // 2, lax.rem(col, 2)

    def wrap(i):
        return lax.rem(i + 2 * N, N)

    def device(axis, step):
        if axis == "x":
            return (wrap(x + step), col, y)
        if axis == "y":
            return (x, col, wrap(y + step))
        return (x, wrap(z + step) * 2 + core, y)

    sibling = (x, z * 2 + 1 - core, y)

    barrier = pltpu.get_barrier_semaphore()
    partners = [sibling]
    partners += [device("y", s) for s in range(1, N)] + [device("z", s) for s in range(1, N)]
    partners += [device("x", s) for s in (1, -1, 2, -2)]
    for partner in partners:
        pl.semaphore_signal(barrier, inc=1, device_id=partner, device_id_type=MESH)
    loads = [
        pltpu.make_async_copy(occ_hbm, occ_raw, load_sem.at[6]),
        pltpu.make_async_copy(virt_hbm, virt_raw, load_sem.at[7]),
    ] + [pltpu.make_async_copy(x_hbm.at[p], x_raw.at[p], load_sem.at[p]) for p in range(6)]
    for load in loads:
        load.start()

    loads[0].wait()
    n_block = 2 * x + y // 4
    n_living = (lax.rem(y, 4) * 32 + lax.broadcasted_iota(jnp.int32, (32, 128), 0)) < sizes[n_block]
    k_living = lax.broadcasted_iota(jnp.int32, (32, 128), 1) < sizes[col]
    o_keep = n_living & k_living & (occ_mask[n_block, col] > 0)
    og[x, y] = jnp.where(o_keep, occ_raw[...].astype(jnp.float32), 0.0).astype(jnp.bfloat16)
    loads[1].wait()
    m_block = 2 * x + col // 8
    m_living = (lax.rem(col, 8) * 16 + lax.broadcasted_iota(jnp.int32, (16, 128), 0)) < sizes[m_block]
    lane = lax.broadcasted_iota(jnp.int32, (16, 128), 1)
    for half in range(2):
        a_block = 2 * y + half
        v_keep = m_living & (lane < sizes[a_block]) & (virt_mask[a_block, m_block] > 0)
        part = virt_raw[:, half * 128 : half * 128 + 128].astype(jnp.float32)
        vs[z, :, half * 128 : half * 128 + 128] = jnp.where(v_keep, part, 0.0).astype(jnp.bfloat16)
    keep = [jnp.where(pair_mask[2 * y + half, col] > 0, 1.0, 0.0).astype(jnp.bfloat16) for half in range(2)]
    for p in range(6):
        loads[2 + p].wait()
        if p < 3:
            for half in range(2):
                rows = pl.ds(half * 128, 128)
                xa[p, 0, core, rows] = x_raw[p, rows] * keep[half]
        else:
            for half in range(2):
                part = x_raw[p, pl.ds(half * 128, 128)] * keep[half]
                xb[p - 3, 0, pl.ds(half * 4, 4)] = part.reshape(4, 2, 16, 128)

    pl.semaphore_wait(barrier, len(partners))

    started = []

    def start(copy):
        copy.start()
        started.append(copy)
        return copy

    def remote(src, dst, send, recv, to):
        return start(pltpu.make_async_remote_copy(
            src_ref=src, dst_ref=dst, send_sem=send, recv_sem=recv, device_id=to, device_id_type=MESH))

    def window(buf, p, place, half):
        if buf is xa or buf is gb:
            ref = buf.at[p, place, core]
            return ref if half is None else ref.at[pl.ds(half * 128, 128)]
        ref = buf.at[p, place]
        return ref if half is None else ref.at[pl.ds(half * 4, 4)]

    class Gather:
        def __init__(self, index, axis, buf, p):
            self.index, self.axis, self.buf, self.p = index, axis, buf, p
            self.copies = {}

        def send(self, way, edge):
            step = 1 - 2 * way
            at, to = EDGES[edge]
            half = way if to == 4 else None
            self.copies[way, edge] = remote(
                window(self.buf, self.p, PLACE[-step * at], half),
                window(self.buf, self.p, PLACE[-step * to], half),
                ring_send.at[self.index, way, edge],
                ring_recv.at[self.index, way, edge],
                device(self.axis, step * (to - at)),
            )

        def arrived(self, way, edge):
            self.copies[way, edge].wait_recv()

    class Density:
        def __init__(self, index):
            self.index, self.copies = index, {}

        def send(self, way, edge):
            step = 1 - 2 * way
            at, to = EDGES[edge]
            group = wrap(x - step * at)
            ref = og.at[group] if self.index == 0 else vg.at[group, core]
            if to == 4:
                ref = ref.at[pl.ds(way * (4 if self.index == 0 else 128), 4 if self.index == 0 else 128)]
            self.copies[way, edge] = remote(
                ref, ref, dens_send.at[self.index, way, edge], dens_recv.at[self.index, way, edge],
                device("x", step * (to - at)))

        def arrived(self, way, edge):
            self.copies[way, edge].wait_recv()

    def share(buf, p, index, stage):
        first, count = ((0, 1), (1, 2), (3, 2), (5, 3))[stage]
        ref = buf.at[p, pl.ds(first, count), core]
        return remote(ref, ref, sib_send.at[index, stage], sib_recv.at[index, stage], sibling)

    def share_virt(i, group):
        ref = vg.at[group, core]
        return remote(ref, ref, vsib_send.at[i], vsib_recv.at[i], sibling)

    first = []
    for s in (4, 3, -3, 2, -2, 1, -1):
        slot = s % N
        first.append(remote(og.at[x, y], og.at[x, y], first_send.at[0, slot], first_recv.at[0, slot], device("y", s)))
        first.append(remote(vs.at[z], vs.at[z], first_send.at[1, slot], first_recv.at[1, slot], device("z", s)))

    phase1 = []
    for p in range(3):
        phase1 += [Gather(2 * p, "z", xa, p), Gather(2 * p + 1, "y", xb, p)]
    shares = {}

    for g in phase1:
        for way in range(2):
            g.send(way, 0)
    for g in phase1:
        if g.buf is xa:
            shares[g.index, 0] = share(xa, g.p, g.index, 0)

    for g in phase1:
        for way in range(2):
            g.arrived(way, 0)
            g.send(way, 1)
        if g.buf is xa:
            shares[g.index, 1] = share(xa, g.p, g.index, 1)

    for copy in first:
        copy.wait_recv()
    vg[x, core] = vs[...].reshape(128, 256).T
    dens = [Density(0), Density(1)]
    for way in range(2):
        for d in dens:
            d.send(way, 0)
    vshares = [share_virt(0, x)]

    for g in phase1:
        for way in range(2):
            g.arrived(way, 1)
            g.send(way, 2)
            g.send(way, 3)
        if g.buf is xa:
            shares[g.index, 2] = share(xa, g.p, g.index, 2)

    for way in range(2):
        for d in dens:
            d.arrived(way, 0)
            d.send(way, 1)
        vshares.append(share_virt(1 + way, wrap(x - (1 - 2 * way))))
    for way in range(2):
        for d in dens:
            d.arrived(way, 1)
            d.send(way, 2)
            d.send(way, 3)
        vshares.append(share_virt(3 + way, wrap(x - 2 * (1 - 2 * way))))

    for g in phase1:
        for way in range(2):
            g.arrived(way, 2)
        for way in range(2):
            g.arrived(way, 3)
        if g.buf is xa:
            shares[g.index, 3] = share(xa, g.p, g.index, 3)

    for way in range(2):
        for d in dens:
            d.arrived(way, 2)
        vshares.append(share_virt(5 + way, wrap(x - 3 * (1 - 2 * way))))
    for way in range(2):
        for d in dens:
            d.arrived(way, 3)
    vshares.append(share_virt(7, wrap(x + 4)))

    def times_occ(buf, p):
        total = jnp.zeros((256, 128), jnp.float32)
        for place in range(N):
            group = wrap(z + RELATIVE[place])
            left = jnp.concatenate([buf[p, place, 0], buf[p, place, 1]], axis=1)
            total += jnp.dot(left, og[group].reshape(256, 128), preferred_element_type=jnp.float32)
        return total.astype(jnp.bfloat16)

    def virt_times(buf, p):
        total = jnp.zeros((256, 128), jnp.float32)
        for place in range(N):
            group = wrap(y + RELATIVE[place])
            left = jnp.concatenate([vg[group, 0], vg[group, 1]], axis=1)
            right = jnp.concatenate(
                [buf[p, place, :, 0].reshape(128, 128), buf[p, place, :, 1].reshape(128, 128)], axis=0)
            total += jnp.dot(left, right, preferred_element_type=jnp.float32)
        return total.astype(jnp.bfloat16)

    phase2 = []
    for p in range(3):
        phase2 += [Gather(6 + 2 * p, "y", ha, p), Gather(7 + 2 * p, "z", gb, p)]
    for g in phase2:
        if g.buf is ha:
            for stage in range(4):
                shares[2 * g.p, stage].wait_recv()
            ha[g.p, 0] = times_occ(xa, g.p).reshape(8, 2, 16, 128)
        else:
            if g.p == 0:
                for copy in vshares:
                    copy.wait_recv()
            gb[g.p, 0, core] = virt_times(xb, g.p)
        for way in range(2):
            g.send(way, 0)
        if g.buf is gb:
            shares[g.index, 0] = share(gb, g.p, g.index - 1, 0)
    for g in phase2:
        for way in range(2):
            g.arrived(way, 0)
            g.send(way, 1)
        if g.buf is gb:
            shares[g.index, 1] = share(gb, g.p, g.index - 1, 1)
    for g in phase2:
        for way in range(2):
            g.arrived(way, 1)
            g.send(way, 2)
            g.send(way, 3)
        if g.buf is gb:
            shares[g.index, 2] = share(gb, g.p, g.index - 1, 2)
    stores = []
    for g in phase2:
        for way in range(2):
            g.arrived(way, 2)
        for way in range(2):
            g.arrived(way, 3)
        if g.buf is gb:
            shares[g.index, 3] = share(gb, g.p, g.index - 1, 3)
        else:
            outs[g.p] = virt_times(ha, g.p)
            store = pltpu.make_async_copy(outs.at[g.p], out_hbm.at[g.p], store_sem.at[g.p])
            store.start()
            stores.append(store)
    for g in phase2:
        if g.buf is gb:
            for stage in range(4):
                shares[g.index, stage].wait_recv()
            outs[3 + g.p] = times_occ(gb, g.p)
            store = pltpu.make_async_copy(outs.at[3 + g.p], out_hbm.at[3 + g.p], store_sem.at[3 + g.p])
            store.start()
            stores.append(store)
    for copy in started:
        copy.wait_send()
    for store in stores:
        store.wait()


def on_device(three_centre, occ_density, virt_density, pair_mask, occ_mask, virt_mask, block_sizes):
    bf16 = jnp.bfloat16
    any_space = pl.BlockSpec(memory_space=pl.ANY)
    scalars = pl.BlockSpec(memory_space=pltpu.SMEM)
    dma = pltpu.SemaphoreType.DMA
    edges = len(EDGES)
    out = pl.pallas_call(
        kernel,
        out_shape=jax.ShapeDtypeStruct((6, 256, 128), bf16),
        in_specs=[any_space] * 3 + [scalars] * 4,
        out_specs=any_space,
        scratch_shapes=[
            pltpu.VMEM((6, 256, 128), bf16),
            pltpu.VMEM((32, 128), bf16),
            pltpu.VMEM((16, 256), bf16),
            pltpu.VMEM((3, N, 2, 256, 128), bf16),
            pltpu.VMEM((3, N, 8, 2, 16, 128), bf16),
            pltpu.VMEM((3, N, 8, 2, 16, 128), bf16),
            pltpu.VMEM((3, N, 2, 256, 128), bf16),
            pltpu.VMEM((N, 8, 32, 128), bf16),
            pltpu.VMEM((N, 16, 256), bf16),
            pltpu.VMEM((N, 2, 256, 128), bf16),
            pltpu.VMEM((6, 256, 128), bf16),
            dma((8,)),
            dma((6,)),
            dma((2, N)),
            dma((2, N)),
            dma((2, 2, edges)),
            dma((2, 2, edges)),
            dma((12, 2, edges)),
            dma((12, 2, edges)),
            dma((12, 4)),
            dma((12, 4)),
            dma((N,)),
            dma((N,)),
        ],
        compiler_params=pltpu.CompilerParams(
            collective_id=0, has_side_effects=True, vmem_limit_bytes=32 << 20
        ),
        cost_estimate=pl.CostEstimate(flops=1610612736, bytes_accessed=1 << 20, transcendentals=0),
        name="transform",
    )(
        jnp.transpose(three_centre, (1, 0, 2)), occ_density.T, virt_density.T,
        pair_mask, occ_mask, virt_mask, block_sizes,
    )
    return jnp.transpose(out, (1, 0, 2))


def solution(mesh):
    placed = (
        P("layer", "row", "col"),
        P("col", ("row", "layer")),
        P("layer", ("row", "col")),
        P(),
        P(),
        P(),
        P(),
    )
    return jax.shard_map(
        on_device, mesh=mesh, in_specs=placed, out_specs=P("layer", "row", "col"), check_vma=False
    )
```

time: 233 us -> 81.3 us (0.35)
  waiting for transfers between devices: 160 us -> 0 us
  Pallas kernels: 0 us -> 75 us
  blocking collectives: 41.8 us -> 0 us
  matrix products: 14.9 us -> 0 us
  between operations: 13.2 us -> 0.02 us
  local copies, waits for them, and re-layouts: 0 us -> 5.88 us
  other arithmetic: 2.97 us -> 0 us
    all_gather x3 -> x0, waiting for transfers between devices: 160 us -> none  [the longest x1 81.9 us: on_device(): virt_rows = lax.all_gather(virt_shard, ('row', 'col'), axis=1, tiled=True)]
    pallas_call x0 -> x1, Pallas kernels: none -> 75 us  [on_device(): pl.pallas_call(kernel, out_shape=jax.ShapeDtypeStruct((6, 256, 128), bf16...]
    all_gather x1 -> x0, blocking collectives: 41.8 us -> none  [on_device(): occ_rows = lax.all_gather(occ_shard, ('row', 'layer'), axis=1, tiled=True)]
    dot_general x8 -> x0, matrix products: 14.9 us -> none  [the longest x1 5.33 us: on_device(): jnp.einsum('mpn,kn->mpk', lax.all_gather(pair_data, 'col', axis=2, tiled=...]
    unnamed x0 -> x15, local copies, waits for them, and re-layouts: none -> 5.88 us
  transfers between devices with their start and end apart: 3 -> 0, of which waited for: 3 -> 0; matrix products, arithmetic and copies ran while one was open for 5% -> 0% of each run, Pallas kernels for 0% -> 0%
where the time goes in v1:
time: 81.3 us; the launch traced here: 80.9 us
  Pallas kernels  75 us (92%)
  local copies, waits for them, and re-layouts  5.88 us (7%)
    pallas_call x1, Pallas kernels, on_device(): pl.pallas_call(kernel, out_shape=jax.ShapeDtypeStruct((6, 256, 128), bf16...  75 us
    unnamed x15, local copies, waits for them, and re-layouts  5.88 us

profile of v1, /device:TPU:1, one launch (start us, length us, event | category | flops | bytes accessed | tf_op | source)
XLA Modules:
  0.0 80.9 jit_solution(8870895877196650222)
XLA Ops:
  0.0 0.0 copy-start.6
  0.0 0.7 copy-done.6
  0.7 0.0 copy-start
  0.7 1.0 %copy-done = bf16[256,6,128]{2,0,1:T(8,128)(2,1)S(1)} copy-done((bf16[256,6,128]{2,0,1:T(8,128)(2,1)S(1)}, bf16[256,6,128]{2,0,1:T(8,128)(2,1)}, u32[]{:S(2)}) %copy-start) | copy-done | bytes 393240
  1.7 0.0 copy-start.1
  1.7 0.7 copy-done.1
  2.4 0.0 copy-start.2
  2.4 0.7 copy-done.2
  3.0 0.0 copy-start.3
  3.0 0.7 copy-done.3
  3.7 0.0 copy-start.4
  3.7 0.7 copy-done.4
  4.4 0.0 copy-start.5
  4.4 0.7 copy-done.5
  5.1 75.0 %transform.1 = bf16[6,256,128]{2,1,0:T(8,128)(2,1)S(1)} custom-call(bf16[6,256,128]{2,1,0:T(8,128)(2,1)S(1)} %bitcast.5, bf16[32,128]{1,0:T(8,128)(2,1)S(1)} %bitcast.6, bf16[16,256]{1,0:T(8,128)(2,1)S(1)} %bitcast.7, s32[16,16]{1,0:T(8,128)S(1)} %copy-done.3, s32[16,16]{1,0:T(8,128)S(1)} %copy-done.4, s32[16,16]{1,0:T(8,128)S(1)} %copy-done.5, s32[16]{0:T(128)S(1)} %copy-done.6), custom_call_target="tpu_custom_call" | custom-call | flops 1610612736 | bytes 1048576 | tf_op jit(solution)/shard_map/transform/pallas_call | solution.py:298
  80.2 0.7 copy.9
Async XLA Ops:
  0.0 0.7 copy-start.6
  0.7 1.0 %copy-start = (bf16[256,6,128]{2,0,1:T(8,128)(2,1)S(1)}, bf16[256,6,128]{2,0,1:T(8,128)(2,1)}, u32[]{:S(2)}) copy-start(bf16[256,6,128]{2,0,1:T(8,128)(2,1)} %param.7) | copy-start | bytes 1179652
  1.7 0.7 copy-start.1
  2.4 0.7 copy-start.2
  3.0 0.7 copy-start.3
  3.7 0.7 copy-start.4
  4.4 0.7 copy-start.5

commit v2 on v1

v2 whole, which is shorter than its diff:
```python
import jax
import jax.numpy as jnp
from jax import lax
from jax.experimental import pallas as pl
from jax.experimental.pallas import tpu as pltpu
from jax.sharding import PartitionSpec as P

MESH = pl.DeviceIdType.MESH
BLOCK = 128
N = 8
RELATIVE = (0, -1, 1, -2, 2, -3, 3, 4)
PLACE = {0: 0, -1: 1, 1: 2, -2: 3, 2: 4, -3: 5, 3: 6, 4: 7, -4: 7}
STAGES = (((0, 1),), ((1, 2),), ((2, 3), (2, 4)))
EDGES = tuple(edge for stage in STAGES for edge in stage)
STAGE_OF = ((0,), (1,), (2, 3))


def kernel(
    x_hbm, occ_hbm, virt_hbm, pair_hbm, occ_mask_hbm, virt_mask_hbm, sizes_hbm,
    out_hbm,
    pair_mask, occ_mask, virt_mask, sizes,
    x_raw, occ_raw, virt_raw, xa, xb, ha, gb, og, og_other, vs, vg, mine, give, got, outs,
    load_sem, store_sem, first_send, first_recv, dens_send, dens_recv,
    ring_send, ring_recv, part_send, part_recv, sib_send, sib_recv,
):
    x, col, y = lax.axis_index("row"), lax.axis_index("col"), lax.axis_index("layer")
    z, core = col // 2, lax.rem(col, 2)

    def wrap(i):
        return lax.rem(i + 2 * N, N)

    def device(axis, step):
        if axis == "x":
            return (wrap(x + step), col, y)
        if axis == "y":
            return (x, col, wrap(y + step))
        return (x, wrap(z + step) * 2 + core, y)

    sibling = (x, z * 2 + 1 - core, y)

    barrier = pltpu.get_barrier_semaphore()
    partners = [sibling]
    partners += [device("y", s) for s in range(1, N)] + [device("z", s) for s in range(1, N)]
    partners += [device("x", s) for s in (1, -1, 2, -2)]
    for partner in partners:
        pl.semaphore_signal(barrier, inc=1, device_id=partner, device_id_type=MESH)
    pairs = (
        (sizes_hbm, sizes), (occ_mask_hbm, occ_mask), (virt_mask_hbm, virt_mask), (pair_hbm, pair_mask),
        (occ_hbm, occ_raw), (virt_hbm, virt_raw),
    ) + tuple((x_hbm.at[p], x_raw.at[p]) for p in range(6))
    loads = [pltpu.make_async_copy(src, dst, load_sem.at[i]) for i, (src, dst) in enumerate(pairs)]
    for load in loads:
        load.start()

    for load in loads[:5]:
        load.wait()
    n_block = 2 * x + y // 4
    n_living = (lax.rem(y, 4) * 32 + lax.broadcasted_iota(jnp.int32, (32, 128), 0)) < sizes[n_block]
    k_living = lax.broadcasted_iota(jnp.int32, (32, 128), 1) < sizes[col]
    o_keep = n_living & k_living & (occ_mask[n_block, col] > 0)
    og[x, y] = jnp.where(o_keep, occ_raw[...].astype(jnp.float32), 0.0).astype(jnp.bfloat16)
    loads[5].wait()
    m_block = 2 * x + col // 8
    m_living = (lax.rem(col, 8) * 16 + lax.broadcasted_iota(jnp.int32, (16, 128), 0)) < sizes[m_block]
    lane = lax.broadcasted_iota(jnp.int32, (16, 128), 1)
    for half in range(2):
        a_block = 2 * y + half
        v_keep = m_living & (lane < sizes[a_block]) & (virt_mask[a_block, m_block] > 0)
        part = virt_raw[:, half * 128 : half * 128 + 128].astype(jnp.float32)
        vs[z, :, half * 128 : half * 128 + 128] = jnp.where(v_keep, part, 0.0).astype(jnp.bfloat16)
    keep = [jnp.where(pair_mask[2 * y + half, col] > 0, 1.0, 0.0).astype(jnp.bfloat16) for half in range(2)]
    for p in range(6):
        loads[6 + p].wait()
        if p < 3:
            for half in range(2):
                rows = pl.ds(half * 128, 128)
                xa[p, 0, rows] = x_raw[p, rows] * keep[half]
        else:
            for half in range(2):
                part = x_raw[p, pl.ds(half * 128, 128)] * keep[half]
                xb[p - 3, 0, pl.ds(half * 4, 4)] = part.reshape(4, 2, 16, 128)

    pl.semaphore_wait(barrier, len(partners))

    started = []

    class Flight:
        def __init__(self, copy):
            self.copy, self.waited = copy, False
            copy.start()
            started.append(self)

        def wait_recv(self):
            if not self.waited:
                self.copy.wait_recv()
            self.waited = True

    def remote(src, dst, send, recv, to):
        return Flight(pltpu.make_async_remote_copy(
            src_ref=src, dst_ref=dst, send_sem=send, recv_sem=recv, device_id=to, device_id_type=MESH))

    def window(buf, p, place, half):
        ref = buf.at[p, place]
        if half is None:
            return ref
        return ref.at[pl.ds(half * 128, 128)] if buf is xa or buf is gb else ref.at[pl.ds(half * 4, 4)]

    class Gather:
        def __init__(self, index, axis, buf, p):
            self.index, self.axis, self.buf, self.p = index, axis, buf, p
            self.copies = {}

        def send(self, way, edge):
            step = 1 - 2 * way
            at, to = EDGES[edge]
            half = way if to == 4 else None
            self.copies[way, edge] = remote(
                window(self.buf, self.p, PLACE[-step * at], half),
                window(self.buf, self.p, PLACE[-step * to], half),
                ring_send.at[self.index, way, edge],
                ring_recv.at[self.index, way, edge],
                device(self.axis, step * (to - at)),
            )

        def advance(self, stage):
            for way in range(2):
                if stage > 0:
                    self.copies[way, STAGE_OF[stage - 1][0]].wait_recv()
                for edge in STAGE_OF[stage]:
                    self.send(way, edge)

        def finish(self):
            for copy in self.copies.values():
                copy.wait_recv()

    class Density(Gather):
        def __init__(self, index):
            self.index, self.copies = index, {}

        def send(self, way, edge):
            step = 1 - 2 * way
            at, to = EDGES[edge]
            group = wrap(x - step * at)
            ref = og.at[group] if self.index == 0 else vg.at[group, core]
            if to == 4:
                half = 4 if self.index == 0 else 128
                ref = ref.at[pl.ds(way * half, half)]
            self.copies[way, edge] = remote(
                ref, ref, dens_send.at[self.index, way, edge], dens_recv.at[self.index, way, edge],
                device("x", step * (to - at)))

    from_sibling = []

    def share(place):
        group = wrap(x + RELATIVE[place])
        ref = vg.at[group, core]
        from_sibling.append(remote(ref, ref, sib_send.at[1, place], sib_recv.at[1, place], sibling))
        from_sibling.append(remote(
            og.at[group, pl.ds(4 - 4 * core, 4)], og_other.at[group],
            sib_send.at[0, place], sib_recv.at[0, place], sibling))

    first = []
    for s in (4, 3, -3, 2, -2, 1, -1):
        slot = s % N
        first.append(remote(og.at[x, y], og.at[x, y], first_send.at[0, slot], first_recv.at[0, slot], device("y", s)))
        first.append(remote(vs.at[z], vs.at[z], first_send.at[1, slot], first_recv.at[1, slot], device("z", s)))
    phase1 = []
    for p in range(3):
        phase1 += [Gather(2 * p, "z", xa, p), Gather(2 * p + 1, "y", xb, p)]
    dens = [Density(0), Density(1)]
    for g in phase1:
        g.advance(0)

    for copy in first:
        copy.wait_recv()
    vg[x, core] = vs[...].reshape(128, 256).T
    for d in dens:
        d.advance(0)
    share(0)
    for g in phase1:
        g.advance(1)
    for d in dens:
        d.advance(1)
    share(1)
    share(2)
    for g in phase1:
        g.advance(2)
    for d in dens:
        d.advance(2)
    share(3)
    share(4)
    for d in dens:
        d.finish()
    for place in (5, 6, 7):
        share(place)
    for copy in from_sibling:
        copy.wait_recv()
    for g in phase1:
        g.finish()

    def occ_rows(group):
        own = og[group, pl.ds(4 * core, 4)].reshape(128, 128)
        return jnp.concatenate([own, og_other[group].reshape(128, 128)], axis=1)

    def times_occ(buf, p):
        total = jnp.zeros((256, 256), jnp.float32)
        for place in range(0, N, 2):
            left = jnp.concatenate([buf[p, place], buf[p, place + 1]], axis=1)
            right = jnp.concatenate([occ_rows(wrap(z + RELATIVE[place + i])) for i in range(2)], axis=0)
            total += jnp.dot(left, right, preferred_element_type=jnp.float32)
        return total

    def virt_times(buf, p):
        total = jnp.zeros((256, 128), jnp.float32)
        for place in range(N):
            group = wrap(y + RELATIVE[place])
            left = jnp.concatenate([vg[group, 0], vg[group, 1]], axis=1)
            right = jnp.concatenate(
                [buf[p, place, :, 0].reshape(128, 128), buf[p, place, :, 1].reshape(128, 128)], axis=0)
            total += jnp.dot(left, right, preferred_element_type=jnp.float32)
        return total.astype(jnp.bfloat16)

    def hand_over(buf, p, index):
        total = times_occ(buf, p)
        mine[index] = total[:, :128]
        give[index] = total[:, 128:]
        return remote(give.at[index], got.at[index], part_send.at[index], part_recv.at[index], sibling)

    phase2, parts = [], []
    for p in range(3):
        phase2 += [Gather(6 + 2 * p, "z", gb, p), Gather(7 + 2 * p, "y", ha, p)]
    for p in range(3):
        parts.append(hand_over(xa, p, p))
        gb[p, 0] = virt_times(xb, p)
        phase2[2 * p].advance(0)
        parts[p].wait_recv()
        ha[p, 0] = (mine[p] + got[p]).astype(jnp.bfloat16).reshape(8, 2, 16, 128)
        phase2[2 * p + 1].advance(0)
    for g in phase2:
        g.advance(1)
    for g in phase2:
        g.advance(2)
    stores = []

    def put(p, value):
        outs[p] = value
        stores.append(pltpu.make_async_copy(outs.at[p], out_hbm.at[p], store_sem.at[p]))
        stores[-1].start()

    for p in range(3):
        phase2[2 * p].finish()
        parts.append(hand_over(gb, p, 3 + p))
        phase2[2 * p + 1].finish()
        put(p, virt_times(ha, p))
        parts[3 + p].wait_recv()
        put(3 + p, (mine[3 + p] + got[3 + p]).astype(jnp.bfloat16))
    for flight in started:
        flight.copy.wait_send()
    for store in stores:
        store.wait()


def on_device(three_centre, occ_density, virt_density, pair_mask, occ_mask, virt_mask, block_sizes):
    bf16 = jnp.bfloat16
    any_space = pl.BlockSpec(memory_space=pl.ANY)
    dma = pltpu.SemaphoreType.DMA
    edges = len(EDGES)
    out = pl.pallas_call(
        kernel,
        out_shape=jax.ShapeDtypeStruct((6, 256, 128), bf16),
        in_specs=[any_space] * 7,
        out_specs=any_space,
        scratch_shapes=[
            pltpu.SMEM((16, 16), jnp.int32),
            pltpu.SMEM((16, 16), jnp.int32),
            pltpu.SMEM((16, 16), jnp.int32),
            pltpu.SMEM((16,), jnp.int32),
            pltpu.VMEM((6, 256, 128), bf16),
            pltpu.VMEM((32, 128), bf16),
            pltpu.VMEM((16, 256), bf16),
            pltpu.VMEM((3, N, 256, 128), bf16),
            pltpu.VMEM((3, N, 8, 2, 16, 128), bf16),
            pltpu.VMEM((3, N, 8, 2, 16, 128), bf16),
            pltpu.VMEM((3, N, 256, 128), bf16),
            pltpu.VMEM((N, 8, 32, 128), bf16),
            pltpu.VMEM((N, 4, 32, 128), bf16),
            pltpu.VMEM((N, 16, 256), bf16),
            pltpu.VMEM((N, 2, 256, 128), bf16),
            pltpu.VMEM((6, 256, 128), jnp.float32),
            pltpu.VMEM((6, 256, 128), jnp.float32),
            pltpu.VMEM((6, 256, 128), jnp.float32),
            pltpu.VMEM((6, 256, 128), bf16),
            dma((12,)),
            dma((6,)),
            dma((2, N)),
            dma((2, N)),
            dma((2, 2, edges)),
            dma((2, 2, edges)),
            dma((12, 2, edges)),
            dma((12, 2, edges)),
            dma((6,)),
            dma((6,)),
            dma((2, N)),
            dma((2, N)),
        ],
        compiler_params=pltpu.CompilerParams(
            collective_id=0, has_side_effects=True, vmem_limit_bytes=60 << 20
        ),
        cost_estimate=pl.CostEstimate(flops=1610612736, bytes_accessed=1 << 20, transcendentals=0),
        name="transform",
    )(
        jnp.transpose(three_centre, (1, 0, 2)), occ_density.T, virt_density.T,
        pair_mask, occ_mask, virt_mask, block_sizes,
    )
    return jnp.transpose(out, (1, 0, 2))


def solution(mesh):
    placed = (
        P("layer", "row", "col"),
        P("col", ("row", "layer")),
        P("layer", ("row", "col")),
        P(),
        P(),
        P(),
        P(),
    )
    return jax.shard_map(
        on_device, mesh=mesh, in_specs=placed, out_specs=P("layer", "row", "col"), check_vma=False
    )
```

time: 81.3 us -> 71.5 us (0.88)
  Pallas kernels: 75 us -> 69.5 us
  local copies, waits for them, and re-layouts: 5.88 us -> 1.77 us
    pallas_call x1, Pallas kernels: 75 us -> 69.5 us  [on_device(): pl.pallas_call(kernel, out_shape=jax.ShapeDtypeStruct((6, 256, 128), bf16...]
    unnamed x15 -> x1, local copies, waits for them, and re-layouts: 5.88 us -> 1.77 us
where the time goes in v2:
time: 71.5 us; the launch traced here: 71.3 us
  Pallas kernels  69.5 us (97%)
  local copies, waits for them, and re-layouts  1.77 us (2%)
    pallas_call x1, Pallas kernels, on_device(): pl.pallas_call(kernel, out_shape=jax.ShapeDtypeStruct((6, 256, 128), bf16...  69.5 us
    unnamed x1, local copies, waits for them, and re-layouts  1.77 us

profile of v2, /device:TPU:1, one launch (start us, length us, event | category | flops | bytes accessed | tf_op | source)
XLA Modules:
  0.0 71.3 jit_solution(12947654722427827281)
XLA Ops:
  0.0 69.5 %transform.1 = bf16[6,256,128]{2,1,0:T(8,128)(2,1)} custom-call(bf16[6,256,128]{2,1,0:T(8,128)(2,1)} %bitcast.5, bf16[32,128]{1,0:T(8,128)(2,1)} %bitcast.6, bf16[16,256]{1,0:T(8,128)(2,1)} %bitcast.7, s32[16,16]{1,0:T(8,128)} %pair_hbm.1, s32[16,16]{1,0:T(8,128)} %occ_mask_hbm.1, s32[16,16]{1,0:T(8,128)} %virt_mask_hbm.1, s32[16]{0:T(128)} %sizes_hbm.1), custom_call_target="tpu_custom_call" | custom-call | flops 1610612736 | bytes 1048576 | tf_op jit(solution)/shard_map/transform/pallas_call | solution.py:268
  69.5 1.8 %copy.9 = bf16[256,6,128]{2,0,1:T(8,128)(2,1)} copy(bf16[256,6,128]{2,0,1:T(8,128)(2,1)} %bitcast.4) | data formatting | bytes 786432

commit v3 on v2

v3 whole, which is shorter than its diff:
```python
import functools

import jax
import jax.numpy as jnp
from jax import lax
from jax.experimental import pallas as pl
from jax.experimental.pallas import tpu as pltpu
from jax.sharding import PartitionSpec as P

MESH = pl.DeviceIdType.MESH
BLOCK = 128
N = 8
RELATIVE = (0, -1, 1, -2, 2, -3, 3, 4)
PLACE = {0: 0, -1: 1, 1: 2, -2: 3, 2: 4, -3: 5, 3: 6, 4: 7, -4: 7}
TREE = (((0, 1),), ((1, 2),), ((2, 3), (2, 4)))
ARRIVALS = {(1, 0): 0, (1, 1): 1, (2, 0): 2, (2, 1): 3, (3, 0): 4, (3, 1): 4, (4, 0): 4, (4, 1): 4}
LAST = 4

def kernel(
    x_hbm, occ_hbm, virt_hbm, pair_hbm, occ_mask_hbm, virt_mask_hbm, sizes_hbm,
    out_hbm,
    pair_mask, occ_mask, virt_mask, sizes,
    x_raw, occ_raw, virt_raw, xa, xb, ha, gb, og, og_other, vs, vg, mine, give, got, held, outs,
    load_sem, store_sem, first_send, first_recv, dens_send, dens_recv,
    ring_send, ring_recv, part_send, part_recv, sib_send, sib_recv,
):
    x, col, y = lax.axis_index("row"), lax.axis_index("col"), lax.axis_index("layer")
    z, core = col // 2, lax.rem(col, 2)

    def wrap(i):
        return lax.rem(i + 2 * N, N)

    def device(axis, step):
        if axis == "x":
            return (wrap(x + step), col, y)
        if axis == "y":
            return (x, col, wrap(y + step))
        return (x, wrap(z + step) * 2 + core, y)

    sibling = (x, z * 2 + 1 - core, y)

    pairs = (
        (sizes_hbm, sizes), (occ_mask_hbm, occ_mask), (virt_mask_hbm, virt_mask), (pair_hbm, pair_mask),
        (occ_hbm, occ_raw), (virt_hbm, virt_raw), (x_hbm, x_raw),
    )
    loads = [pltpu.make_async_copy(src, dst, load_sem.at[i]) for i, (src, dst) in enumerate(pairs)]
    for load in loads:
        load.start()
    barrier = pltpu.get_barrier_semaphore()
    partners = [sibling]
    partners += [device("y", s) for s in range(1, N)] + [device("z", s) for s in range(1, N)]
    partners += [device("x", s) for s in (1, -1, 2, -2)]
    for partner in partners:
        pl.semaphore_signal(barrier, inc=1, device_id=partner, device_id_type=MESH)

    for load in loads[:5]:
        load.wait()
    n_block = 2 * x + y // 4
    n_living = (lax.rem(y, 4) * 32 + lax.broadcasted_iota(jnp.int32, (32, 128), 0)) < sizes[n_block]
    k_living = lax.broadcasted_iota(jnp.int32, (32, 128), 1) < sizes[col]
    o_keep = n_living & k_living & (occ_mask[n_block, col] > 0)
    og[x, y] = jnp.where(o_keep, occ_raw[...].astype(jnp.float32), 0.0).astype(jnp.bfloat16)
    loads[5].wait()
    m_block = 2 * x + col // 8
    m_living = (lax.rem(col, 8) * 16 + lax.broadcasted_iota(jnp.int32, (16, 128), 0)) < sizes[m_block]
    lane = lax.broadcasted_iota(jnp.int32, (16, 128), 1)
    for half in range(2):
        a_block = 2 * y + half
        v_keep = m_living & (lane < sizes[a_block]) & (virt_mask[a_block, m_block] > 0)
        part = virt_raw[:, half * 128 : half * 128 + 128].astype(jnp.float32)
        vs[z, :, half * 128 : half * 128 + 128] = jnp.where(v_keep, part, 0.0).astype(jnp.bfloat16)
    pl.semaphore_wait(barrier, len(partners))

    def remote(src, dst, send, recv, to):
        copy = pltpu.make_async_remote_copy(
            src_ref=src, dst_ref=dst, send_sem=send, recv_sem=recv, device_id=to, device_id_type=MESH)
        copy.start()
        return copy

    def wait_bytes(ref, sem):
        pltpu.make_async_copy(ref, ref, sem).wait()

    def window(buf, p, place, half):
        ref = buf.at[p, place]
        if half is None:
            return ref
        return ref.at[pl.ds(half * 128, 128)] if buf is xa or buf is gb else ref.at[pl.ds(half * 4, 4)]

    class Gather:
        def __init__(self, index, axis, buf, p):
            self.index, self.axis, self.buf, self.p, self.copies = index, axis, buf, p, {}

        def send(self, way, at, to):
            step = 1 - 2 * way
            half = way if to == 4 else None
            self.copies[way, to] = remote(
                window(self.buf, self.p, PLACE[-step * at], half),
                window(self.buf, self.p, PLACE[-step * to], half),
                ring_send.at[self.index // 3],
                ring_recv.at[self.index, ARRIVALS[to, way]],
                device(self.axis, step * (to - at)),
            )

        def advance(self, stage):
            for way in range(2):
                if stage > 0:
                    self.copies[way, stage].wait_recv()
                for at, to in TREE[stage]:
                    self.send(way, at, to)

        def finish(self):
            wait_bytes(self.buf.at[self.p, pl.ds(5, 3)], ring_recv.at[self.index, LAST])

    class Density(Gather):
        def __init__(self, index):
            self.index, self.copies = index, {}

        def send(self, way, at, to):
            step = 1 - 2 * way
            group = wrap(x - step * at)
            ref = og.at[group] if self.index == 0 else vg.at[group, core]
            if to == 4:
                half = 4 if self.index == 0 else 128
                ref = ref.at[pl.ds(way * half, half)]
            self.copies[way, to] = remote(
                ref, ref, dens_send.at[self.index], dens_recv.at[self.index, ARRIVALS[to, way]],
                device("x", step * (to - at)))

        def finish(self):
            ref = og.at[pl.ds(0, 3)] if self.index == 0 else vg.at[pl.ds(0, 3), 0]
            wait_bytes(ref, dens_recv.at[self.index, LAST])

    def share(place):
        group = wrap(x + RELATIVE[place])
        ref, late = vg.at[group, core], place // 4
        remote(ref, ref, sib_send.at[1], sib_recv.at[1, late], sibling)
        remote(og.at[group, pl.ds(4 - 4 * core, 4)], og_other.at[group], sib_send.at[0], sib_recv.at[0, late], sibling)

    def shared_arrived(late):
        wait_bytes(og_other.at[pl.ds(0, 4)], sib_recv.at[0, late])
        wait_bytes(vg.at[pl.ds(0, 4), 0], sib_recv.at[1, late])

    def first_step():
        for s in (4, 3, -3, 2, -2, 1, -1):
            remote(og.at[x, y], og.at[x, y], first_send.at[0], first_recv.at[0], device("y", s))
            remote(vs.at[z], vs.at[z], first_send.at[1], first_recv.at[1], device("z", s))

    dens = [Density(0), Density(1)]

    def groups_ready():
        wait_bytes(og.at[x, pl.ds(0, 7)], first_recv.at[0])
        dens[0].advance(0)
        wait_bytes(vs.at[pl.ds(0, 7)], first_recv.at[1])
        vg[x, core] = vs[...].reshape(128, 256).T
        dens[1].advance(0)
        share(0)

    def groups_pass(stage):
        for d in dens:
            d.advance(stage)
        share(2 * stage - 1)
        share(2 * stage)

    def groups_done():
        for d in dens:
            d.finish()
        for place in (5, 6, 7):
            share(place)

    def occ_rows(group):
        own = og[group, pl.ds(4 * core, 4)].reshape(128, 128)
        return jnp.concatenate([own, og_other[group].reshape(128, 128)], axis=1)

    def place_of(group, here):
        apart = wrap(group - here)
        return jnp.minimum(2 * apart, 15 - 2 * apart)

    def times_occ(buf, p, pairs):
        left = jnp.concatenate([buf[p, place] for place, _ in pairs], axis=1)
        right = jnp.concatenate([occ_rows(group) for _, group in pairs], axis=0)
        return jnp.dot(left, right, preferred_element_type=jnp.float32)

    def virt_times(buf, p, pairs):
        left = jnp.concatenate([vg[group, half] for _, group in pairs for half in range(2)], axis=1)
        right = jnp.concatenate(
            [buf[p, place, :, half].reshape(128, 128) for place, _ in pairs for half in range(2)], axis=0)
        return jnp.dot(left, right, preferred_element_type=jnp.float32)

    def occ_early(buf, p, index, pairs):
        total = times_occ(buf, p, pairs)
        mine[index] = total[:, :128]
        give[index] = total[:, 128:]

    def occ_late(buf, p, index, pairs):
        total = times_occ(buf, p, pairs)
        give[index] += total[:, 128:]
        parts[index] = remote(give.at[index], got.at[index], part_send.at[0], part_recv.at[index], sibling)
        mine[index] += total[:, :128]

    def occ_total(index):
        parts[index].wait_recv()
        return (mine[index] + got[index]).astype(jnp.bfloat16)

    def virt_early(buf, p, index, pairs):
        held[index] = virt_times(buf, p, pairs)

    def virt_late(buf, p, index, pairs):
        return (held[index] + virt_times(buf, p, pairs)).astype(jnp.bfloat16)

    parts = {}
    by_group = [wrap(x + RELATIVE[i]) for i in range(N)]
    occ1 = [(place_of(group, z), group) for group in by_group]
    virt1 = [(place_of(group, y), group) for group in by_group]
    occ2 = [(i, wrap(z + RELATIVE[i])) for i in range(N)]
    virt2 = [(i, wrap(y + RELATIVE[i])) for i in range(N)]
    phase1 = [(Gather(p, "z", xa, p), Gather(3 + p, "y", xb, p)) for p in range(3)]
    phase2 = [(Gather(6 + p, "z", gb, p), Gather(9 + p, "y", ha, p)) for p in range(3)]

    def both(p, stage):
        for g in phase1[p]:
            g.advance(stage)

    def shards_done():
        for pair in phase1:
            for g in pair:
                g.finish()

    def early():
        for p in range(3):
            occ_early(xa, p, p, occ1[:4])
            virt_early(xb, p, p, virt1[:4])

    first_step()
    loads[6].wait()
    keep = [jnp.where(pair_mask[2 * y + half, col] > 0, 1.0, 0.0).astype(jnp.bfloat16) for half in range(2)]
    for p in range(3):
        for half in range(2):
            rows = pl.ds(half * 128, 128)
            xa[p, 0, rows] = x_raw[p, rows] * keep[half]
            xb[p, 0, pl.ds(half * 4, 4)] = (x_raw[3 + p, rows] * keep[half]).reshape(4, 2, 16, 128)
        both(p, 0)
    tasks = [(4.2, groups_ready)]
    for p in range(3):
        for stage in range(1, len(TREE)):
            tasks.append((3.6 + 0.8 * p + 3.2 * (stage - 1), functools.partial(both, p, stage)))
    for stage in range(1, len(TREE)):
        tasks.append((7.5 + 3.3 * (stage - 1), functools.partial(groups_pass, stage)))
    for _, task in sorted(tasks, key=lambda entry: entry[0]):
        task()
    shards_done()
    shared_arrived(0)
    early()
    groups_done()
    shared_arrived(1)

    def begin_b(p):
        gb[p, 0] = virt_late(xb, p, p, virt1[4:])
        phase2[p][0].advance(0)

    def begin_a(p):
        ha[p, 0] = occ_total(p).reshape(8, 2, 16, 128)
        phase2[p][1].advance(0)

    for p in range(3):
        occ_late(xa, p, p, occ1[4:])
    for p in range(3):
        begin_b(p)
        begin_a(p)
    for stage in range(1, len(TREE)):
        for p in range(3):
            for g in phase2[p]:
                g.advance(stage)
    for p in range(3):
        occ_early(gb, p, 3 + p, occ2[:4])
        virt_early(ha, p, 3 + p, virt2[:4])
    def put(p, value):
        outs[p] = value
        pltpu.make_async_copy(outs.at[p], out_hbm.at[p], store_sem.at[0]).start()

    for p in range(3):
        phase2[p][0].finish()
        occ_late(gb, p, 3 + p, occ2[4:])
        phase2[p][1].finish()
        put(p, virt_late(ha, p, 3 + p, virt2[4:]))
        put(3 + p, occ_total(3 + p))
    for i, buf in enumerate((xa, xb, gb, ha)):
        wait_bytes(buf.at[:, pl.ds(0, 7)], ring_send.at[i])
    wait_bytes(og.at[pl.ds(0, 7)], dens_send.at[0])
    wait_bytes(vg.at[pl.ds(0, 7), 0], dens_send.at[1])
    wait_bytes(og.at[0, pl.ds(0, 7)], first_send.at[0])
    wait_bytes(vs.at[pl.ds(0, 7)], first_send.at[1])
    wait_bytes(og_other, sib_send.at[0])
    wait_bytes(vg.at[:, 0], sib_send.at[1])
    wait_bytes(give, part_send.at[0])
    wait_bytes(outs, store_sem.at[0])


def on_device(three_centre, occ_density, virt_density, pair_mask, occ_mask, virt_mask, block_sizes):
    bf16 = jnp.bfloat16
    any_space = pl.BlockSpec(memory_space=pl.ANY)
    dma = pltpu.SemaphoreType.DMA
    out = pl.pallas_call(
        kernel,
        out_shape=jax.ShapeDtypeStruct((6, 256, 128), bf16),
        in_specs=[any_space] * 7,
        out_specs=any_space,
        scratch_shapes=[
            pltpu.SMEM((16, 16), jnp.int32),
            pltpu.SMEM((16, 16), jnp.int32),
            pltpu.SMEM((16, 16), jnp.int32),
            pltpu.SMEM((16,), jnp.int32),
            pltpu.VMEM((6, 256, 128), bf16),
            pltpu.VMEM((32, 128), bf16),
            pltpu.VMEM((16, 256), bf16),
            pltpu.VMEM((3, N, 256, 128), bf16),
            pltpu.VMEM((3, N, 8, 2, 16, 128), bf16),
            pltpu.VMEM((3, N, 8, 2, 16, 128), bf16),
            pltpu.VMEM((3, N, 256, 128), bf16),
            pltpu.VMEM((N, 8, 32, 128), bf16),
            pltpu.VMEM((N, 4, 32, 128), bf16),
            pltpu.VMEM((N, 16, 256), bf16),
            pltpu.VMEM((N, 2, 256, 128), bf16),
            pltpu.VMEM((6, 256, 128), jnp.float32),
            pltpu.VMEM((6, 256, 128), jnp.float32),
            pltpu.VMEM((6, 256, 128), jnp.float32),
            pltpu.VMEM((6, 256, 128), jnp.float32),
            pltpu.VMEM((6, 256, 128), bf16),
            dma((7,)),
            dma((1,)),
            dma((2,)),
            dma((2,)),
            dma((2,)),
            dma((2, 5)),
            dma((4,)),
            dma((12, 5)),
            dma((1,)),
            dma((6,)),
            dma((2,)),
            dma((2, 2)),
        ],
        compiler_params=pltpu.CompilerParams(
            collective_id=0, has_side_effects=True, vmem_limit_bytes=60 << 20
        ),
        cost_estimate=pl.CostEstimate(flops=1610612736, bytes_accessed=1 << 20, transcendentals=0),
        name="transform",
    )(
        jnp.transpose(three_centre, (1, 0, 2)), occ_density.T, virt_density.T,
        pair_mask, occ_mask, virt_mask, block_sizes,
    )
    return jnp.transpose(out, (1, 0, 2))


def solution(mesh):
    placed = (
        P("layer", "row", "col"),
        P("col", ("row", "layer")),
        P("layer", ("row", "col")),
        P(),
        P(),
        P(),
        P(),
    )
    return jax.shard_map(
        on_device, mesh=mesh, in_specs=placed, out_specs=P("layer", "row", "col"), check_vma=False
    )
```

time: 71.5 us -> 69.7 us (0.975)
  Pallas kernels: 69.5 us -> 67.7 us
    pallas_call x1, Pallas kernels: 69.5 us -> 67.7 us  [on_device(): pl.pallas_call(kernel, out_shape=jax.ShapeDtypeStruct((6, 256, 128), bf16...]
where the time goes in v3:
time: 69.7 us; the launch traced here: 69.5 us
  Pallas kernels  67.7 us (97%)
  local copies, waits for them, and re-layouts  1.77 us (3%)
    pallas_call x1, Pallas kernels, on_device(): pl.pallas_call(kernel, out_shape=jax.ShapeDtypeStruct((6, 256, 128), bf16...  67.7 us
    unnamed x1, local copies, waits for them, and re-layouts  1.77 us

profile of v3, /device:TPU:1, one launch (start us, length us, event | category | flops | bytes accessed | tf_op | source)
XLA Modules:
  0.0 69.5 jit_solution(2624503310781470846)
XLA Ops:
  0.0 67.7 %transform.1 = bf16[6,256,128]{2,1,0:T(8,128)(2,1)} custom-call(bf16[6,256,128]{2,1,0:T(8,128)(2,1)} %bitcast.5, bf16[32,128]{1,0:T(8,128)(2,1)} %bitcast.6, bf16[16,256]{1,0:T(8,128)(2,1)} %bitcast.7, s32[16,16]{1,0:T(8,128)} %pair_hbm.1, s32[16,16]{1,0:T(8,128)} %occ_mask_hbm.1, s32[16,16]{1,0:T(8,128)} %virt_mask_hbm.1, s32[16]{0:T(128)} %sizes_hbm.1), custom_call_target="tpu_custom_call" | custom-call | flops 1610612736 | bytes 1048576 | tf_op jit(solution)/shard_map/transform/pallas_call | solution.py:302
  67.7 1.8 %copy.9 = bf16[256,6,128]{2,0,1:T(8,128)(2,1)} copy(bf16[256,6,128]{2,0,1:T(8,128)(2,1)} %bitcast.4) | data formatting | bytes 786432

commit v4 on v3

--- a/solution.py
+++ b/solution.py
@@ -12,7 +12,7 @@
 N = 8
 RELATIVE = (0, -1, 1, -2, 2, -3, 3, 4)
 PLACE = {0: 0, -1: 1, 1: 2, -2: 3, 2: 4, -3: 5, 3: 6, 4: 7, -4: 7}
-TREE = (((0, 1),), ((1, 2),), ((2, 3), (2, 4)))
+TREE = (((0, 1),), ((1, 2),), ((2, 4), (2, 3)))
 ARRIVALS = {(1, 0): 0, (1, 1): 1, (2, 0): 2, (2, 1): 3, (3, 0): 4, (3, 1): 4, (4, 0): 4, (4, 1): 4}
 LAST = 4
 
@@ -123,12 +123,11 @@
                 half = 4 if self.index == 0 else 128
                 ref = ref.at[pl.ds(way * half, half)]
             self.copies[way, to] = remote(
-                ref, ref, dens_send.at[self.index], dens_recv.at[self.index, ARRIVALS[to, way]],
+                ref, ref, dens_send.at[self.index], dens_recv.at[self.index, 2 * to - 2 + way if to < 4 else 6],
                 device("x", step * (to - at)))
 
         def finish(self):
-            ref = og.at[pl.ds(0, 3)] if self.index == 0 else vg.at[pl.ds(0, 3), 0]
-            wait_bytes(ref, dens_recv.at[self.index, LAST])
+            wait_bytes(og.at[0] if self.index == 0 else vg.at[0, 0], dens_recv.at[self.index, 6])
 
     def share(place):
         group = wrap(x + RELATIVE[place])
@@ -162,10 +161,13 @@
         share(2 * stage)
 
     def groups_done():
+        for way in range(2):
+            for d in dens:
+                d.copies[way, 3].wait_recv()
+            share(5 + way)
         for d in dens:
             d.finish()
-        for place in (5, 6, 7):
-            share(place)
+        share(7)
 
     def occ_rows(group):
         own = og[group, pl.ds(4 * core, 4)].reshape(128, 128)
@@ -330,7 +332,7 @@
             dma((2,)),
             dma((2,)),
             dma((2,)),
-            dma((2, 5)),
+            dma((2, 7)),
             dma((4,)),
             dma((12, 5)),
             dma((1,)),

time: 69.7 us -> 69.8 us (level)
  no operation moved by 1% of the time
where the time goes in v4:
time: 69.8 us; the launch traced here: 69.6 us
  Pallas kernels  67.8 us (97%)
  local copies, waits for them, and re-layouts  1.77 us (3%)
    pallas_call x1, Pallas kernels, on_device(): pl.pallas_call(kernel, out_shape=jax.ShapeDtypeStruct((6, 256, 128), bf16...  67.8 us
    unnamed x1, local copies, waits for them, and re-layouts  1.77 us

profile of v4, /device:TPU:1, one launch (start us, length us, event | category | flops | bytes accessed | tf_op | source)
XLA Modules:
  0.0 69.6 jit_solution(2682824501894192207)
XLA Ops:
  0.0 67.8 %transform.1 = bf16[6,256,128]{2,1,0:T(8,128)(2,1)} custom-call(bf16[6,256,128]{2,1,0:T(8,128)(2,1)} %bitcast.5, bf16[32,128]{1,0:T(8,128)(2,1)} %bitcast.6, bf16[16,256]{1,0:T(8,128)(2,1)} %bitcast.7, s32[16,16]{1,0:T(8,128)} %pair_hbm.1, s32[16,16]{1,0:T(8,128)} %occ_mask_hbm.1, s32[16,16]{1,0:T(8,128)} %virt_mask_hbm.1, s32[16]{0:T(128)} %sizes_hbm.1), custom_call_target="tpu_custom_call" | custom-call | flops 1610612736 | bytes 1048576 | tf_op jit(solution)/shard_map/transform/pallas_call | solution.py:304
  67.8 1.8 %copy.9 = bf16[256,6,128]{2,0,1:T(8,128)(2,1)} copy(bf16[256,6,128]{2,0,1:T(8,128)(2,1)} %bitcast.4) | data formatting | bytes 786432
